TPU v7x, 256 devices: a whole 4x4x8 slice. The times are simulated.
256 devices in a mesh: shot: 4 (over x), space: 64 (over z, y, core).
Axes of the slice: x: 4, y: 4, z: 8, core: 2. Of those that a mesh axis runs over, the one named last changes fastest.
Arguments:
- model_velocity: float32 [2, 64, 4, 256, 128], P(None, 'space'), may hold values from 1.5 to 4.5
- first_tile: int32 [4], P('shot'), may hold values from 0 to 64
- src_weight: float32 [8, 256, 256], P('shot', 'space'), may hold values from -6 to 6
- src_depth: int32 [8, 256, 256], P('shot', 'space'), may hold values from 0 to 127
- wavelet: float32 [8, 4], P('shot'), may hold values from -0.6 to 0.6
- rec_depth: int32 [8, 256, 256], P('shot', 'space'), may hold values from 0 to 127
- residual: float32 [8, 4, 256, 256], P('shot', None, 'space'), may hold values from -0.6 to 0.6
Outputs:
- gradient: float32 [2, 64, 4, 256, 128], P(None, 'space', 'shot')
Inputs may be any that keep to these rules, and one draw needn't show every extreme that they name: Group g's aperture is the 64 consecutive model tiles starting at first_tile[g].
All inputs are finite; a program needn't handle non-finite values.
Results may differ from a plain program's by a relative error of at most 0.0001.
Values sent between devices are 32-bit elements; how exact they have to be, the bound alone decides.
No kernel may reach another device: no remote copies, remote signals or barrier semaphores. Data moves between devices by JAX's collectives and lax.ppermute only.
A program may use at most 64 MiB of HBM per device.

v0:
```python
import jax
import jax.numpy as jnp
from jax import lax
from jax.sharding import PartitionSpec as P

COEFS = (-205.0 / 72.0, 8.0 / 5.0, -1.0 / 5.0, 8.0 / 315.0, -1.0 / 560.0)


def from_behind(value, axis, steps):
    count = lax.axis_size(axis)
    pairs = [(source, (source + steps) % count) for source in range(count)]
    return lax.ppermute(value, axis, pairs)


def extended(array, sides, width):
    for axis, dim in sides:
        size, length = (lax.axis_size(axis), array.shape[dim])
        up = [(i, (i + 1) % size) for i in range(size - 1)]
        down = [(j, i) for i, j in up]
        last = lax.slice_in_dim(array, length - width, length, axis=dim)
        initial = lax.slice_in_dim(array, 0, width, axis=dim)
        before = lax.ppermute(last, axis, up)
        after = lax.ppermute(initial, axis, down)
        array = jnp.concatenate([before, array, after], axis=dim)
    return array


def lap_local(padded_x):
    full = jnp.pad(padded_x, ((0, 0), (0, 0), (4, 4), (4, 4)))
    size_x = full.shape[1] - 8
    size_y = full.shape[2] - 8
    size_z = full.shape[3] - 8
    center = full[:, 4 : 4 + size_x, 4 : 4 + size_y, 4 : 4 + size_z]
    total = 3.0 * COEFS[0] * center
    for step in range(1, 5):
        beside_all = full[:, 4 + step : 4 + step + size_x, 4 : 4 + size_y, 4 : 4 + size_z]
        beside_all = (
            beside_all + full[:, 4 - step : 4 - step + size_x, 4 : 4 + size_y, 4 : 4 + size_z]
        )
        beside_all = (
            beside_all + full[:, 4 : 4 + size_x, 4 + step : 4 + step + size_y, 4 : 4 + size_z]
        )
        beside_all = (
            beside_all + full[:, 4 : 4 + size_x, 4 - step : 4 - step + size_y, 4 : 4 + size_z]
        )
        beside_all = (
            beside_all + full[:, 4 : 4 + size_x, 4 : 4 + size_y, 4 + step : 4 + step + size_z]
        )
        beside_all = (
            beside_all + full[:, 4 : 4 + size_x, 4 : 4 + size_y, 4 - step : 4 - step + size_z]
        )
        total = total + COEFS[step] * beside_all
    return total


def rotate_steps(tile, amount):
    count = lax.axis_size("space").bit_length() - 1
    for bit in range(count):
        moved = from_behind(tile, "space", 1 << bit)
        tile = jnp.where(amount // (1 << bit) % 2 == 1, moved, tile)
    return tile


def move_tile(tile, amount):
    return rotate_steps(tile, amount)


def body(model_velocity, first_tile, src_weight, src_depth, wavelet, rec_depth, residual):
    width = lax.axis_size("space")
    place = lax.axis_index("space")
    anchor = first_tile[0]
    offset = anchor % width
    lowest = anchor // width
    slot = jnp.where(place >= offset, lowest, lowest + 1)
    owned = lax.dynamic_index_in_dim(model_velocity, slot, 0, keepdims=False)[0]
    velocity = move_tile(owned, (width - offset) % width)
    coeff = (0.1 * velocity) ** 2
    depth = lax.broadcasted_iota(jnp.int32, (1, 1, 1, velocity.shape[2]), 3)
    source = jnp.where(
        depth == src_depth[..., None], src_weight[..., None], jnp.zeros((), jnp.float32)
    )
    probe = jnp.where(
        depth == rec_depth[..., None], jnp.ones((), jnp.float32), jnp.zeros((), jnp.float32)
    )
    start = jnp.zeros(source.shape, jnp.float32)

    def forward(carry, amplitude):
        before, now = carry
        padded = extended(now, (("space", 1),), 4)
        lap_now = lap_local(padded)
        after = 2.0 * now - before + coeff * lap_now + amplitude[:, None, None, None] * source
        return ((now, after), lap_now)

    _, laps = lax.scan(forward, (start, start), jnp.transpose(wavelet))
    traces = jnp.moveaxis(jnp.flip(residual, 1), 1, 0)

    def adjoint(carry, items):
        before, now, image = carry
        lap_fwd, trace = items
        padded = extended(now, (("space", 1),), 4)
        after = 2.0 * now - before + coeff * lap_local(padded) + trace[..., None] * probe
        return ((now, after, image + after * lap_fwd), None)

    (_, _, image), _ = lax.scan(adjoint, (start, start, start), (jnp.flip(laps, 0), traces))
    local_grad = 0.02 * velocity * jnp.sum(image, 0)
    returned = move_tile(local_grad, offset)
    slab = jnp.zeros(model_velocity.shape, jnp.float32)
    slab = lax.dynamic_update_index_in_dim(slab, returned[None], slot, 0)
    return lax.psum_scatter(slab, "shot", scatter_dimension=2, tiled=True)


def solution(mesh):
    placed = (
        P(None, "space", None, None, None),
        P("shot"),
        P("shot", "space", None),
        P("shot", "space", None),
        P("shot", None),
        P("shot", "space", None),
        P("shot", None, "space", None),
    )
    return jax.shard_map(
        body,
        mesh=mesh,
        in_specs=placed,
        out_specs=P(None, "space", "shot", None, None),
        check_vma=False,
    )
```

profile of v0, /device:TPU:1, one launch (start us, length us, event | category | flops | bytes accessed | tf_op | source)
XLA Modules:
  0.0 662.9 jit_solution(5838120420366856394)
XLA Ops:
  8.4 2.8 collective-permute-start.4
  11.1 6.1 collective-permute-done.4
  19.7 11.4 %collective-permute-done.5 = f32[4,256,128]{2,1,0:T(8,128)S(1)} collective-permute-done((f32[4,256,128]{2,1,0:T(8,128)S(1)}, f32[4,256,128]{2,1,0:T(8,128)S(1)}, u32[]{:S(2)}, u32[]{:S(2)}) %collective-permute-start.5) | collective-permute-done | bytes 524320 | tf_op jit(solution)/shard_map/ppermute | solution.py:12
  33.0 11.9 %collective-permute-done.6 = f32[4,256,128]{2,1,0:T(8,128)S(1)} collective-permute-done((f32[4,256,128]{2,1,0:T(8,128)S(1)}, f32[4,256,128]{2,1,0:T(8,128)S(1)}, u32[]{:S(2)}, u32[]{:S(2)}) %collective-permute-start.6) | collective-permute-done | bytes 524320 | tf_op jit(solution)/shard_map/ppermute | solution.py:12
  45.1 9.4 %collective-permute-done.7 = f32[4,256,128]{2,1,0:T(8,128)S(1)} collective-permute-done((f32[4,256,128]{2,1,0:T(8,128)S(1)}, f32[4,256,128]{2,1,0:T(8,128)S(1)}, u32[]{:S(2)}, u32[]{:S(2)}) %collective-permute-start.7) | collective-permute-done | bytes 524320 | tf_op jit(solution)/shard_map/ppermute | solution.py:12
  54.5 4.7 collective-permute-start.8
  59.2 10.2 %collective-permute-done.8 = f32[4,256,128]{2,1,0:T(8,128)S(1)} collective-permute-done((f32[4,256,128]{2,1,0:T(8,128)S(1)}, f32[4,256,128]{2,1,0:T(8,128)S(1)}, u32[]{:S(2)}, u32[]{:S(2)}) %collective-permute-start.8) | collective-permute-done | bytes 524320 | tf_op jit(solution)/shard_map/ppermute | solution.py:12
  69.5 3.5 collective-permute-start.9
  73.1 26.1 %collective-permute-done.9 = f32[4,256,128]{2,1,0:T(8,128)S(1)} collective-permute-done((f32[4,256,128]{2,1,0:T(8,128)S(1)}, f32[4,256,128]{2,1,0:T(8,128)S(1)}, u32[]{:S(2)}, u32[]{:S(2)}) %collective-permute-start.9) | collective-permute-done | bytes 524320 | tf_op jit(solution)/shard_map/ppermute | solution.py:12
  101.2 153.8 %while.34 = (s32[]{:T(128)}, f32[2,4,256,128]{3,2,1,0:T(8,128)}, f32[2,4,256,128]{3,2,1,0:T(8,128)}, f32[4,2,4,256,128]{4,3,2,1,0:T(8,128)}, f32[4,256,128]{2,1,...) while((s32[]{:T(128)}, f32[2,4,256,128]{3,2,1,0:T(8,128)}, ...), condition=%wide.region_1.2_spmd.clone, body=%wide.region_0.1_spmd.clone.sunk | while | flops 24721924 | bytes 45930724 | solution.py:94
  101.3 13.4 %collective-permute-start = (f32[2,4,256,128]{3,2,1,0:T(8,128)S(1)}, f32[2,4,256,128]{3,2,1,0:T(8,128)}, u32[]{:S(2)}, u32[]{:S(2)}) collective-permute-start(f32[2,4,256,128]{3,2,1,0:T(8,128)S(1)} %broadcast_select_fusion.15), channel_id=1, source_target_pairs={{1,0},{2,1},{3,2},{4,3},{5,4},{6,5},{7,6},{8,7},{9,8},{10,9},{11,1... | collective-permute-start | bytes 3145736 | tf_op jit(solution)/shard_map/while/body/eval_jaxpr/ppermute | solution.py:23
  114.8 8.3 %collective-permute-start.1 = (f32[2,4,256,128]{3,2,1,0:T(8,128)S(1)}, f32[2,4,256,128]{3,2,1,0:T(8,128)}, u32[]{:S(2)}, u32[]{:S(2)}) collective-permute-start(f32[2,4,256,128]{3,2,1,0:T(8,128)S(1)} %broadcast_select_fusion.15), channel_id=1, source_target_pairs={{0,1},{1,2},{2,3},{3,4},{4,5},{5,6},{6,7},{7,8},{8,9},{9,10},{10,1... | collective-permute-start | bytes 3145736 | tf_op jit(solution)/shard_map/while/body/eval_jaxpr/ppermute | solution.py:22
  123.1 10.6 %collective-permute-done = f32[2,4,256,128]{3,2,1,0:T(8,128)} collective-permute-done((f32[2,4,256,128]{3,2,1,0:T(8,128)S(1)}, f32[2,4,256,128]{3,2,1,0:T(8,128)}, u32[]{:S(2)}, u32[]{:S(2)}) %collective-permute-start) | collective-permute-done | bytes 1048608 | tf_op jit(solution)/shard_map/while/body/eval_jaxpr/ppermute | solution.py:23
  134.8 4.2 select_maximum_fusion.6
  139.0 7.2 %bitcast_dynamic-update-slice_fusion.3 = (f32[4,2,4,256,128]{4,3,2,1,0:T(8,128)}, f32[2,4,256,128]{3,2,1,0:T(8,128)}) fusion(f32[4,2,4,256,128]{4,3,2,1,0:T(8,128)} %get-tuple-element.413, s32[]{:T(128)S(6)} %copy.19, f32[2,12,264,136]{3,2,1,0:T(8,128)S(1)} %select_maximum_fusion.6, f32[2,4,256,128]{3,2,1,0:T(8,128)} %collective-permute-done, ...), kind=kLoop, calls=%fused_computation.52.clone.1 | loop fusion | flops 9175040 | bytes 22020100 | tf_op jit(solution)/shard_map/while/body/jit(dynamic_update_index_in_dim)/dynamic_update_slice | solution.py:94
  146.2 2.9 fusion.65
  151.3 1.9 collective-permute-start
  153.2 4.5 collective-permute-start.1
  157.8 10.6 %collective-permute-done = f32[2,4,256,128]{3,2,1,0:T(8,128)} collective-permute-done((f32[2,4,256,128]{3,2,1,0:T(8,128)S(1)}, f32[2,4,256,128]{3,2,1,0:T(8,128)}, u32[]{:S(2)}, u32[]{:S(2)}) %collective-permute-start) | collective-permute-done | bytes 1048608 | tf_op jit(solution)/shard_map/while/body/eval_jaxpr/ppermute | solution.py:23
  169.5 4.2 select_maximum_fusion.6
  173.7 7.2 %bitcast_dynamic-update-slice_fusion.3 = (f32[4,2,4,256,128]{4,3,2,1,0:T(8,128)}, f32[2,4,256,128]{3,2,1,0:T(8,128)}) fusion(f32[4,2,4,256,128]{4,3,2,1,0:T(8,128)} %get-tuple-element.413, s32[]{:T(128)S(6)} %copy.19, f32[2,12,264,136]{3,2,1,0:T(8,128)S(1)} %select_maximum_fusion.6, f32[2,4,256,128]{3,2,1,0:T(8,128)} %collective-permute-done, ...), kind=kLoop, calls=%fused_computation.52.clone.1 | loop fusion | flops 9175040 | bytes 22020100 | tf_op jit(solution)/shard_map/while/body/jit(dynamic_update_index_in_dim)/dynamic_update_slice | solution.py:94
  180.8 3.2 fusion.65
  186.3 1.9 collective-permute-start
  188.2 4.5 collective-permute-start.1
  192.8 10.6 %collective-permute-done = f32[2,4,256,128]{3,2,1,0:T(8,128)} collective-permute-done((f32[2,4,256,128]{3,2,1,0:T(8,128)S(1)}, f32[2,4,256,128]{3,2,1,0:T(8,128)}, u32[]{:S(2)}, u32[]{:S(2)}) %collective-permute-start) | collective-permute-done | bytes 1048608 | tf_op jit(solution)/shard_map/while/body/eval_jaxpr/ppermute | solution.py:23
  204.5 4.2 select_maximum_fusion.6
  208.7 7.2 %bitcast_dynamic-update-slice_fusion.3 = (f32[4,2,4,256,128]{4,3,2,1,0:T(8,128)}, f32[2,4,256,128]{3,2,1,0:T(8,128)}) fusion(f32[4,2,4,256,128]{4,3,2,1,0:T(8,128)} %get-tuple-element.413, s32[]{:T(128)S(6)} %copy.19, f32[2,12,264,136]{3,2,1,0:T(8,128)S(1)} %select_maximum_fusion.6, f32[2,4,256,128]{3,2,1,0:T(8,128)} %collective-permute-done, ...), kind=kLoop, calls=%fused_computation.52.clone.1 | loop fusion | flops 9175040 | bytes 22020100 | tf_op jit(solution)/shard_map/while/body/jit(dynamic_update_index_in_dim)/dynamic_update_slice | solution.py:94
  215.8 3.2 fusion.65
  221.3 1.9 collective-permute-start
  223.2 4.5 collective-permute-start.1
  227.8 10.6 %collective-permute-done = f32[2,4,256,128]{3,2,1,0:T(8,128)} collective-permute-done((f32[2,4,256,128]{3,2,1,0:T(8,128)S(1)}, f32[2,4,256,128]{3,2,1,0:T(8,128)}, u32[]{:S(2)}, u32[]{:S(2)}) %collective-permute-start) | collective-permute-done | bytes 1048608 | tf_op jit(solution)/shard_map/while/body/eval_jaxpr/ppermute | solution.py:23
  239.5 4.2 select_maximum_fusion.6
  243.7 7.2 %bitcast_dynamic-update-slice_fusion.3 = (f32[4,2,4,256,128]{4,3,2,1,0:T(8,128)}, f32[2,4,256,128]{3,2,1,0:T(8,128)}) fusion(f32[4,2,4,256,128]{4,3,2,1,0:T(8,128)} %get-tuple-element.413, s32[]{:T(128)S(6)} %copy.19, f32[2,12,264,136]{3,2,1,0:T(8,128)S(1)} %select_maximum_fusion.6, f32[2,4,256,128]{3,2,1,0:T(8,128)} %collective-permute-done, ...), kind=kLoop, calls=%fused_computation.52.clone.1 | loop fusion | flops 9175040 | bytes 22020100 | tf_op jit(solution)/shard_map/while/body/jit(dynamic_update_index_in_dim)/dynamic_update_slice | solution.py:94
  250.8 3.2 fusion.65
  255.0 4.7 rev.9
  260.8 174.5 %while.35 = (s32[]{:T(128)}, f32[2,4,256,128]{3,2,1,0:T(8,128)}, f32[2,4,256,128]{3,2,1,0:T(8,128)}, f32[2,4,256,128]{3,2,1,0:T(8,128)}, f32[4,256,128]{2,1,0:T(...) while((s32[]{:T(128)}, f32[2,4,256,128]{3,2,1,0:T(8,128)}, ...), condition=%wide.region_3.4_spmd.clone, body=%wide.region_2.3_spmd.clone.sunk | while | flops 25246212 | bytes 44898512 | solution.py:104
  260.9 1.9 collective-permute-start.2
  262.8 4.5 collective-permute-start.3
  267.3 10.5 %collective-permute-done.2 = f32[2,4,256,128]{3,2,1,0:T(8,128)S(1)} collective-permute-done((f32[2,4,256,128]{3,2,1,0:T(8,128)S(1)}, f32[2,4,256,128]{3,2,1,0:T(8,128)S(1)}, u32[]{:S(2)}, u32[]{:S(2)}) %collective-permute-start.2) | collective-permute-done | bytes 1048608 | tf_op jit(solution)/shard_map/while/body/eval_jaxpr/ppermute | solution.py:23
  279.0 4.4 select_maximum_fusion.7
  283.4 19.0 %fusion.66 = (f32[2,4,256,128]{3,2,1,0:T(8,128)}, f32[2,4,256,128]{3,2,1,0:T(8,128)}) fusion(f32[2,4,256,128]{3,2,1,0:T(8,128)} %get-tuple-element.443, f32[4,2,4,256,128]{4,3,2,1,0:T(8,128)} %get-tuple-element.456, s32[]{:T(128)S(6)} %copy.31, pred[]{:T(512)S(6)} %compare.127, s32[2,4,256]{2,1,0:T(4,128)S(1)} %get-tuple-element.457, ...), kind=kLoop, calls=%fused_computation.112.clone.1 | loop fusion | flops 12058624 | bytes 25706500 | tf_op jit(solution)/shard_map/while/body/eval_jaxpr/add | solution.py:102
  306.6 4.4 collective-permute-start.3
  311.0 10.5 %collective-permute-done.2 = f32[2,4,256,128]{3,2,1,0:T(8,128)S(1)} collective-permute-done((f32[2,4,256,128]{3,2,1,0:T(8,128)S(1)}, f32[2,4,256,128]{3,2,1,0:T(8,128)S(1)}, u32[]{:S(2)}, u32[]{:S(2)}) %collective-permute-start.2) | collective-permute-done | bytes 1048608 | tf_op jit(solution)/shard_map/while/body/eval_jaxpr/ppermute | solution.py:23
  322.7 4.4 select_maximum_fusion.7
  327.1 19.3 %fusion.66 = (f32[2,4,256,128]{3,2,1,0:T(8,128)}, f32[2,4,256,128]{3,2,1,0:T(8,128)}) fusion(f32[2,4,256,128]{3,2,1,0:T(8,128)} %get-tuple-element.443, f32[4,2,4,256,128]{4,3,2,1,0:T(8,128)} %get-tuple-element.456, s32[]{:T(128)S(6)} %copy.31, pred[]{:T(512)S(6)} %compare.127, s32[2,4,256]{2,1,0:T(4,128)S(1)} %get-tuple-element.457, ...), kind=kLoop, calls=%fused_computation.112.clone.1 | loop fusion | flops 12058624 | bytes 25706500 | tf_op jit(solution)/shard_map/while/body/eval_jaxpr/add | solution.py:102
  350.6 4.4 collective-permute-start.3
  355.0 10.5 %collective-permute-done.2 = f32[2,4,256,128]{3,2,1,0:T(8,128)S(1)} collective-permute-done((f32[2,4,256,128]{3,2,1,0:T(8,128)S(1)}, f32[2,4,256,128]{3,2,1,0:T(8,128)S(1)}, u32[]{:S(2)}, u32[]{:S(2)}) %collective-permute-start.2) | collective-permute-done | bytes 1048608 | tf_op jit(solution)/shard_map/while/body/eval_jaxpr/ppermute | solution.py:23
  366.7 4.4 select_maximum_fusion.7
  371.1 19.3 %fusion.66 = (f32[2,4,256,128]{3,2,1,0:T(8,128)}, f32[2,4,256,128]{3,2,1,0:T(8,128)}) fusion(f32[2,4,256,128]{3,2,1,0:T(8,128)} %get-tuple-element.443, f32[4,2,4,256,128]{4,3,2,1,0:T(8,128)} %get-tuple-element.456, s32[]{:T(128)S(6)} %copy.31, pred[]{:T(512)S(6)} %compare.127, s32[2,4,256]{2,1,0:T(4,128)S(1)} %get-tuple-element.457, ...), kind=kLoop, calls=%fused_computation.112.clone.1 | loop fusion | flops 12058624 | bytes 25706500 | tf_op jit(solution)/shard_map/while/body/eval_jaxpr/add | solution.py:102
  394.6 4.4 collective-permute-start.3
  399.0 10.5 %collective-permute-done.2 = f32[2,4,256,128]{3,2,1,0:T(8,128)S(1)} collective-permute-done((f32[2,4,256,128]{3,2,1,0:T(8,128)S(1)}, f32[2,4,256,128]{3,2,1,0:T(8,128)S(1)}, u32[]{:S(2)}, u32[]{:S(2)}) %collective-permute-start.2) | collective-permute-done | bytes 1048608 | tf_op jit(solution)/shard_map/while/body/eval_jaxpr/ppermute | solution.py:23
  410.8 4.4 select_maximum_fusion.7
  415.1 19.2 %fusion.66 = (f32[2,4,256,128]{3,2,1,0:T(8,128)}, f32[2,4,256,128]{3,2,1,0:T(8,128)}) fusion(f32[2,4,256,128]{3,2,1,0:T(8,128)} %get-tuple-element.443, f32[4,2,4,256,128]{4,3,2,1,0:T(8,128)} %get-tuple-element.456, s32[]{:T(128)S(6)} %copy.31, pred[]{:T(512)S(6)} %compare.127, s32[2,4,256]{2,1,0:T(4,128)S(1)} %get-tuple-element.457, ...), kind=kLoop, calls=%fused_computation.112.clone.1 | loop fusion | flops 12058624 | bytes 25706500 | tf_op jit(solution)/shard_map/while/body/eval_jaxpr/add | solution.py:102
  437.8 2.6 collective-permute-start.10
  440.4 6.1 collective-permute-done.10
  446.7 20.8 %collective-permute-done.11 = f32[4,256,128]{2,1,0:T(8,128)S(1)} collective-permute-done((f32[4,256,128]{2,1,0:T(8,128)S(1)}, f32[4,256,128]{2,1,0:T(8,128)S(1)}, u32[]{:S(2)}, u32[]{:S(2)}) %collective-permute-start.11) | collective-permute-done | bytes 524320 | tf_op jit(solution)/shard_map/ppermute | solution.py:12
  467.9 18.7 %collective-permute-done.12 = f32[4,256,128]{2,1,0:T(8,128)S(1)} collective-permute-done((f32[4,256,128]{2,1,0:T(8,128)S(1)}, f32[4,256,128]{2,1,0:T(8,128)S(1)}, u32[]{:S(2)}, u32[]{:S(2)}) %collective-permute-start.12) | collective-permute-done | bytes 524320 | tf_op jit(solution)/shard_map/ppermute | solution.py:12
  486.7 17.3 %collective-permute-start.13 = (f32[4,256,128]{2,1,0:T(8,128)S(1)}, f32[4,256,128]{2,1,0:T(8,128)S(1)}, u32[]{:S(2)}, u32[]{:S(2)}) collective-permute-start(f32[4,256,128]{2,1,0:T(8,128)S(1)} %broadcast_select_fusion.10), channel_id=1, source_target_pairs={{0,8},{1,9},{2,10},{3,11},{4,12},{5,13},{6,14},{7,15},{8,16},{9,17... | collective-permute-start | bytes 1572872 | tf_op jit(solution)/shard_map/ppermute | solution.py:12
  504.0 8.4 %collective-permute-done.13 = f32[4,256,128]{2,1,0:T(8,128)S(1)} collective-permute-done((f32[4,256,128]{2,1,0:T(8,128)S(1)}, f32[4,256,128]{2,1,0:T(8,128)S(1)}, u32[]{:S(2)}, u32[]{:S(2)}) %collective-permute-start.13) | collective-permute-done | bytes 524320 | tf_op jit(solution)/shard_map/ppermute | solution.py:12
  512.5 17.2 %collective-permute-start.14 = (f32[4,256,128]{2,1,0:T(8,128)S(1)}, f32[4,256,128]{2,1,0:T(8,128)S(1)}, u32[]{:S(2)}, u32[]{:S(2)}) collective-permute-start(f32[4,256,128]{2,1,0:T(8,128)S(1)} %broadcast_select_fusion.11), channel_id=1, source_target_pairs={{0,16},{1,17},{2,18},{3,19},{4,20},{5,21},{6,22},{7,23},{8,24},{9,... | collective-permute-start | bytes 1572872 | tf_op jit(solution)/shard_map/ppermute | solution.py:12
  529.7 14.8 %collective-permute-done.14 = f32[4,256,128]{2,1,0:T(8,128)S(1)} collective-permute-done((f32[4,256,128]{2,1,0:T(8,128)S(1)}, f32[4,256,128]{2,1,0:T(8,128)S(1)}, u32[]{:S(2)}, u32[]{:S(2)}) %collective-permute-start.14) | collective-permute-done | bytes 524320 | tf_op jit(solution)/shard_map/ppermute | solution.py:12
  544.7 16.8 %collective-permute-done.15 = f32[4,256,128]{2,1,0:T(8,128)S(1)} collective-permute-done((f32[4,256,128]{2,1,0:T(8,128)S(1)}, f32[4,256,128]{2,1,0:T(8,128)S(1)}, u32[]{:S(2)}, u32[]{:S(2)}) %collective-permute-start.15) | collective-permute-done | bytes 524320 | tf_op jit(solution)/shard_map/ppermute | solution.py:12
  563.2 90.5 %all-reduce.5.cloned.1.call-done = f32[2,1,4,256,128]{4,3,2,1,0:T(8,128)} async-done(((f32[2,1,4,256,128]{4,3,2,1,0:T(8,128)}), f32[2,1,4,256,128]{4,3,2,1,0:T(8,128)}) %all-reduce.5.cloned.1.call-update) | async-done | bytes 1048592
  653.7 2.3 constant_dynamic-slice_fusion
  (87 shorter events, 44.4 us)
Async XLA Ops:
  6.5 66.5 %copy-start.7 = (f32[2,4]{1,0:T(2,128)S(1)}, f32[2,4]{1,0:T(2,128)}, u32[]{:S(2)}) copy-start(f32[2,4]{1,0:T(2,128)} %param.15) | copy-start | bytes 100
  6.5 66.6 %copy-start.6 = (f32[2,4,4,256]{3,2,1,0:T(4,128)S(1)}, f32[2,4,4,256]{3,2,1,0:T(4,128)}, u32[]{:S(2)}) copy-start(f32[2,4,4,256]{3,2,1,0:T(4,128)} %param.17) | copy-start | bytes 98308
  6.5 94.7 %copy-start.4 = (f32[2,4,256]{2,1,0:T(4,128)S(1)}, f32[2,4,256]{2,1,0:T(4,128)}, u32[]{:S(2)}) copy-start(f32[2,4,256]{2,1,0:T(4,128)} %param.13) | copy-start | bytes 24580
  6.5 94.7 %copy-start.3 = (s32[2,4,256]{2,1,0:T(4,128)S(1)}, s32[2,4,256]{2,1,0:T(4,128)}, u32[]{:S(2)}) copy-start(s32[2,4,256]{2,1,0:T(4,128)} %param.14) | copy-start | bytes 24580
  6.5 647.2 %all-reduce.5.cloned.1.call-start = ((), (), s32[]{:S(2)}) async-start(), calls=%async_computation | async-start | bytes 2097152
  8.4 8.9 %collective-permute-start.4 = (f32[4,256,128]{2,1,0:T(8,128)S(1)}, f32[4,256,128]{2,1,0:T(8,128)S(1)}, u32[]{:S(2)}, u32[]{:S(2)}) collective-permute-start(f32[4,256,128]{2,1,0:T(8,128)S(1)} %dynamic-slice_bitcast_fusion.2), channel_id=1, source_target_pairs={{0,1},{1,2},{2,3},{3,4},{4,5},{5,6},{6,7},{7,8},{8,9},{9,10},{10,1... | collective-permute-start | bytes 1572872 | tf_op jit(solution)/shard_map/ppermute | solution.py:12
  18.4 12.8 %collective-permute-start.5 = (f32[4,256,128]{2,1,0:T(8,128)S(1)}, f32[4,256,128]{2,1,0:T(8,128)S(1)}, u32[]{:S(2)}, u32[]{:S(2)}) collective-permute-start(f32[4,256,128]{2,1,0:T(8,128)S(1)} %broadcast_select_fusion.2), channel_id=1, source_target_pairs={{0,2},{1,3},{2,4},{3,5},{4,6},{5,7},{6,8},{7,9},{8,10},{9,11},{10,... | collective-permute-start | bytes 1572872 | tf_op jit(solution)/shard_map/ppermute | solution.py:12
  31.2 13.6 %collective-permute-start.6 = (f32[4,256,128]{2,1,0:T(8,128)S(1)}, f32[4,256,128]{2,1,0:T(8,128)S(1)}, u32[]{:S(2)}, u32[]{:S(2)}) collective-permute-start(f32[4,256,128]{2,1,0:T(8,128)S(1)} %broadcast_select_fusion.3), channel_id=1, source_target_pairs={{0,4},{1,5},{2,6},{3,7},{4,8},{5,9},{6,10},{7,11},{8,12},{9,13},{1... | collective-permute-start | bytes 1572872 | tf_op jit(solution)/shard_map/ppermute | solution.py:12
  44.9 9.5 %collective-permute-start.7 = (f32[4,256,128]{2,1,0:T(8,128)S(1)}, f32[4,256,128]{2,1,0:T(8,128)S(1)}, u32[]{:S(2)}, u32[]{:S(2)}) collective-permute-start(f32[4,256,128]{2,1,0:T(8,128)S(1)} %broadcast_select_fusion.4), channel_id=1, source_target_pairs={{0,8},{1,9},{2,10},{3,11},{4,12},{5,13},{6,14},{7,15},{8,16},{9,17... | collective-permute-start | bytes 1572872 | tf_op jit(solution)/shard_map/ppermute | solution.py:12
  54.5 14.9 %collective-permute-start.8 = (f32[4,256,128]{2,1,0:T(8,128)S(1)}, f32[4,256,128]{2,1,0:T(8,128)S(1)}, u32[]{:S(2)}, u32[]{:S(2)}) collective-permute-start(f32[4,256,128]{2,1,0:T(8,128)S(1)} %broadcast_select_fusion.5), channel_id=1, source_target_pairs={{0,16},{1,17},{2,18},{3,19},{4,20},{5,21},{6,22},{7,23},{8,24},{9,... | collective-permute-start | bytes 1572872 | tf_op jit(solution)/shard_map/ppermute | solution.py:12
  69.5 31.7 %copy-start = (f32[4,256,128]{2,1,0:T(8,128)}, f32[4,256,128]{2,1,0:T(8,128)S(1)}, u32[]{:S(2)}) copy-start(f32[4,256,128]{2,1,0:T(8,128)S(1)} %broadcast_select_fusion.6) | copy-start | bytes 1572868
  69.5 29.7 %collective-permute-start.9 = (f32[4,256,128]{2,1,0:T(8,128)S(1)}, f32[4,256,128]{2,1,0:T(8,128)S(1)}, u32[]{:S(2)}, u32[]{:S(2)}) collective-permute-start(f32[4,256,128]{2,1,0:T(8,128)S(1)} %broadcast_select_fusion.6), channel_id=1, source_target_pairs={{0,32},{1,33},{2,34},{3,35},{4,36},{5,37},{6,38},{7,39},{8,40},{9,... | collective-permute-start | bytes 1572872 | tf_op jit(solution)/shard_map/ppermute | solution.py:12
  99.2 2.0 copy-start.2
  101.3 32.4 %collective-permute-start = (f32[2,4,256,128]{3,2,1,0:T(8,128)S(1)}, f32[2,4,256,128]{3,2,1,0:T(8,128)}, u32[]{:S(2)}, u32[]{:S(2)}) collective-permute-start(f32[2,4,256,128]{3,2,1,0:T(8,128)S(1)} %broadcast_select_fusion.15), channel_id=1, source_target_pairs={{1,0},{2,1},{3,2},{4,3},{5,4},{6,5},{7,6},{8,7},{9,8},{10,9},{11,1... | collective-permute-start | bytes 3145736 | tf_op jit(solution)/shard_map/while/body/eval_jaxpr/ppermute | solution.py:23
  114.8 20.0 %collective-permute-start.1 = (f32[2,4,256,128]{3,2,1,0:T(8,128)S(1)}, f32[2,4,256,128]{3,2,1,0:T(8,128)}, u32[]{:S(2)}, u32[]{:S(2)}) collective-permute-start(f32[2,4,256,128]{3,2,1,0:T(8,128)S(1)} %broadcast_select_fusion.15), channel_id=1, source_target_pairs={{0,1},{1,2},{2,3},{3,4},{4,5},{5,6},{6,7},{7,8},{8,9},{9,10},{10,1... | collective-permute-start | bytes 3145736 | tf_op jit(solution)/shard_map/while/body/eval_jaxpr/ppermute | solution.py:22
  151.3 17.1 %collective-permute-start = (f32[2,4,256,128]{3,2,1,0:T(8,128)S(1)}, f32[2,4,256,128]{3,2,1,0:T(8,128)}, u32[]{:S(2)}, u32[]{:S(2)}) collective-permute-start(f32[2,4,256,128]{3,2,1,0:T(8,128)S(1)} %broadcast_select_fusion.15), channel_id=1, source_target_pairs={{1,0},{2,1},{3,2},{4,3},{5,4},{6,5},{7,6},{8,7},{9,8},{10,9},{11,1... | collective-permute-start | bytes 3145736 | tf_op jit(solution)/shard_map/while/body/eval_jaxpr/ppermute | solution.py:23
  153.2 16.2 %collective-permute-start.1 = (f32[2,4,256,128]{3,2,1,0:T(8,128)S(1)}, f32[2,4,256,128]{3,2,1,0:T(8,128)}, u32[]{:S(2)}, u32[]{:S(2)}) collective-permute-start(f32[2,4,256,128]{3,2,1,0:T(8,128)S(1)} %broadcast_select_fusion.15), channel_id=1, source_target_pairs={{0,1},{1,2},{2,3},{3,4},{4,5},{5,6},{6,7},{7,8},{8,9},{9,10},{10,1... | collective-permute-start | bytes 3145736 | tf_op jit(solution)/shard_map/while/body/eval_jaxpr/ppermute | solution.py:22
  186.3 17.1 %collective-permute-start = (f32[2,4,256,128]{3,2,1,0:T(8,128)S(1)}, f32[2,4,256,128]{3,2,1,0:T(8,128)}, u32[]{:S(2)}, u32[]{:S(2)}) collective-permute-start(f32[2,4,256,128]{3,2,1,0:T(8,128)S(1)} %broadcast_select_fusion.15), channel_id=1, source_target_pairs={{1,0},{2,1},{3,2},{4,3},{5,4},{6,5},{7,6},{8,7},{9,8},{10,9},{11,1... | collective-permute-start | bytes 3145736 | tf_op jit(solution)/shard_map/while/body/eval_jaxpr/ppermute | solution.py:23
  188.2 16.2 %collective-permute-start.1 = (f32[2,4,256,128]{3,2,1,0:T(8,128)S(1)}, f32[2,4,256,128]{3,2,1,0:T(8,128)}, u32[]{:S(2)}, u32[]{:S(2)}) collective-permute-start(f32[2,4,256,128]{3,2,1,0:T(8,128)S(1)} %broadcast_select_fusion.15), channel_id=1, source_target_pairs={{0,1},{1,2},{2,3},{3,4},{4,5},{5,6},{6,7},{7,8},{8,9},{9,10},{10,1... | collective-permute-start | bytes 3145736 | tf_op jit(solution)/shard_map/while/body/eval_jaxpr/ppermute | solution.py:22
  221.3 17.1 %collective-permute-start = (f32[2,4,256,128]{3,2,1,0:T(8,128)S(1)}, f32[2,4,256,128]{3,2,1,0:T(8,128)}, u32[]{:S(2)}, u32[]{:S(2)}) collective-permute-start(f32[2,4,256,128]{3,2,1,0:T(8,128)S(1)} %broadcast_select_fusion.15), channel_id=1, source_target_pairs={{1,0},{2,1},{3,2},{4,3},{5,4},{6,5},{7,6},{8,7},{9,8},{10,9},{11,1... | collective-permute-start | bytes 3145736 | tf_op jit(solution)/shard_map/while/body/eval_jaxpr/ppermute | solution.py:23
  223.2 16.2 %collective-permute-start.1 = (f32[2,4,256,128]{3,2,1,0:T(8,128)S(1)}, f32[2,4,256,128]{3,2,1,0:T(8,128)}, u32[]{:S(2)}, u32[]{:S(2)}) collective-permute-start(f32[2,4,256,128]{3,2,1,0:T(8,128)S(1)} %broadcast_select_fusion.15), channel_id=1, source_target_pairs={{0,1},{1,2},{2,3},{3,4},{4,5},{5,6},{6,7},{7,8},{8,9},{9,10},{10,1... | collective-permute-start | bytes 3145736 | tf_op jit(solution)/shard_map/while/body/eval_jaxpr/ppermute | solution.py:22
  255.0 5.8 copy-start.5
  260.9 17.0 %collective-permute-start.2 = (f32[2,4,256,128]{3,2,1,0:T(8,128)S(1)}, f32[2,4,256,128]{3,2,1,0:T(8,128)S(1)}, u32[]{:S(2)}, u32[]{:S(2)}) collective-permute-start(f32[2,4,256,128]{3,2,1,0:T(8,128)S(1)} %broadcast_select_fusion.16), channel_id=1, source_target_pairs={{1,0},{2,1},{3,2},{4,3},{5,4},{6,5},{7,6},{8,7},{9,8},{10,9},{11,1... | collective-permute-start | bytes 3145736 | tf_op jit(solution)/shard_map/while/body/eval_jaxpr/ppermute | solution.py:23
  262.8 16.2 %collective-permute-start.3 = (f32[2,4,256,128]{3,2,1,0:T(8,128)S(1)}, f32[2,4,256,128]{3,2,1,0:T(8,128)S(1)}, u32[]{:S(2)}, u32[]{:S(2)}) collective-permute-start(f32[2,4,256,128]{3,2,1,0:T(8,128)S(1)} %broadcast_select_fusion.16), channel_id=1, source_target_pairs={{0,1},{1,2},{2,3},{3,4},{4,5},{5,6},{6,7},{7,8},{8,9},{9,10},{10,1... | collective-permute-start | bytes 3145736 | tf_op jit(solution)/shard_map/while/body/eval_jaxpr/ppermute | solution.py:22
  304.7 16.9 %collective-permute-start.2 = (f32[2,4,256,128]{3,2,1,0:T(8,128)S(1)}, f32[2,4,256,128]{3,2,1,0:T(8,128)S(1)}, u32[]{:S(2)}, u32[]{:S(2)}) collective-permute-start(f32[2,4,256,128]{3,2,1,0:T(8,128)S(1)} %broadcast_select_fusion.16), channel_id=1, source_target_pairs={{1,0},{2,1},{3,2},{4,3},{5,4},{6,5},{7,6},{8,7},{9,8},{10,9},{11,1... | collective-permute-start | bytes 3145736 | tf_op jit(solution)/shard_map/while/body/eval_jaxpr/ppermute | solution.py:23
  306.6 16.1 %collective-permute-start.3 = (f32[2,4,256,128]{3,2,1,0:T(8,128)S(1)}, f32[2,4,256,128]{3,2,1,0:T(8,128)S(1)}, u32[]{:S(2)}, u32[]{:S(2)}) collective-permute-start(f32[2,4,256,128]{3,2,1,0:T(8,128)S(1)} %broadcast_select_fusion.16), channel_id=1, source_target_pairs={{0,1},{1,2},{2,3},{3,4},{4,5},{5,6},{6,7},{7,8},{8,9},{9,10},{10,1... | collective-permute-start | bytes 3145736 | tf_op jit(solution)/shard_map/while/body/eval_jaxpr/ppermute | solution.py:22
  348.7 16.9 %collective-permute-start.2 = (f32[2,4,256,128]{3,2,1,0:T(8,128)S(1)}, f32[2,4,256,128]{3,2,1,0:T(8,128)S(1)}, u32[]{:S(2)}, u32[]{:S(2)}) collective-permute-start(f32[2,4,256,128]{3,2,1,0:T(8,128)S(1)} %broadcast_select_fusion.16), channel_id=1, source_target_pairs={{1,0},{2,1},{3,2},{4,3},{5,4},{6,5},{7,6},{8,7},{9,8},{10,9},{11,1... | collective-permute-start | bytes 3145736 | tf_op jit(solution)/shard_map/while/body/eval_jaxpr/ppermute | solution.py:23
  350.6 16.1 %collective-permute-start.3 = (f32[2,4,256,128]{3,2,1,0:T(8,128)S(1)}, f32[2,4,256,128]{3,2,1,0:T(8,128)S(1)}, u32[]{:S(2)}, u32[]{:S(2)}) collective-permute-start(f32[2,4,256,128]{3,2,1,0:T(8,128)S(1)} %broadcast_select_fusion.16), channel_id=1, source_target_pairs={{0,1},{1,2},{2,3},{3,4},{4,5},{5,6},{6,7},{7,8},{8,9},{9,10},{10,1... | collective-permute-start | bytes 3145736 | tf_op jit(solution)/shard_map/while/body/eval_jaxpr/ppermute | solution.py:22
  392.7 16.9 %collective-permute-start.2 = (f32[2,4,256,128]{3,2,1,0:T(8,128)S(1)}, f32[2,4,256,128]{3,2,1,0:T(8,128)S(1)}, u32[]{:S(2)}, u32[]{:S(2)}) collective-permute-start(f32[2,4,256,128]{3,2,1,0:T(8,128)S(1)} %broadcast_select_fusion.16), channel_id=1, source_target_pairs={{1,0},{2,1},{3,2},{4,3},{5,4},{6,5},{7,6},{8,7},{9,8},{10,9},{11,1... | collective-permute-start | bytes 3145736 | tf_op jit(solution)/shard_map/while/body/eval_jaxpr/ppermute | solution.py:23
  394.6 16.1 %collective-permute-start.3 = (f32[2,4,256,128]{3,2,1,0:T(8,128)S(1)}, f32[2,4,256,128]{3,2,1,0:T(8,128)S(1)}, u32[]{:S(2)}, u32[]{:S(2)}) collective-permute-start(f32[2,4,256,128]{3,2,1,0:T(8,128)S(1)} %broadcast_select_fusion.16), channel_id=1, source_target_pairs={{0,1},{1,2},{2,3},{3,4},{4,5},{5,6},{6,7},{7,8},{8,9},{9,10},{10,1... | collective-permute-start | bytes 3145736 | tf_op jit(solution)/shard_map/while/body/eval_jaxpr/ppermute | solution.py:22
  436.6 125.9 %copy-start.8 = (u32[256]{0:T(256)S(1)}, u32[256]{0:T(256)}, u32[]{:S(2)}) copy-start(u32[256]{0:T(256)} %constant.325) | copy-start | bytes 3076
  437.8 8.7 %collective-permute-start.10 = (f32[4,256,128]{2,1,0:T(8,128)S(1)}, f32[4,256,128]{2,1,0:T(8,128)S(1)}, u32[]{:S(2)}, u32[]{:S(2)}) collective-permute-start(f32[4,256,128]{2,1,0:T(8,128)S(1)} %multiply_multiply_fusion.1), channel_id=1, source_target_pairs={{0,1},{1,2},{2,3},{3,4},{4,5},{5,6},{6,7},{7,8},{8,9},{9,10},{10,1... | collective-permute-start | bytes 1572872 | tf_op jit(solution)/shard_map/ppermute | solution.py:12
  446.5 21.0 %collective-permute-start.11 = (f32[4,256,128]{2,1,0:T(8,128)S(1)}, f32[4,256,128]{2,1,0:T(8,128)S(1)}, u32[]{:S(2)}, u32[]{:S(2)}) collective-permute-start(f32[4,256,128]{2,1,0:T(8,128)S(1)} %broadcast_select_fusion.8), channel_id=1, source_target_pairs={{0,2},{1,3},{2,4},{3,5},{4,6},{5,7},{6,8},{7,9},{8,10},{9,11},{10,... | collective-permute-start | bytes 1572872 | tf_op jit(solution)/shard_map/ppermute | solution.py:12
  467.6 19.0 %collective-permute-start.12 = (f32[4,256,128]{2,1,0:T(8,128)S(1)}, f32[4,256,128]{2,1,0:T(8,128)S(1)}, u32[]{:S(2)}, u32[]{:S(2)}) collective-permute-start(f32[4,256,128]{2,1,0:T(8,128)S(1)} %broadcast_select_fusion.9), channel_id=1, source_target_pairs={{0,4},{1,5},{2,6},{3,7},{4,8},{5,9},{6,10},{7,11},{8,12},{9,13},{1... | collective-permute-start | bytes 1572872 | tf_op jit(solution)/shard_map/ppermute | solution.py:12
  486.7 25.7 %collective-permute-start.13 = (f32[4,256,128]{2,1,0:T(8,128)S(1)}, f32[4,256,128]{2,1,0:T(8,128)S(1)}, u32[]{:S(2)}, u32[]{:S(2)}) collective-permute-start(f32[4,256,128]{2,1,0:T(8,128)S(1)} %broadcast_select_fusion.10), channel_id=1, source_target_pairs={{0,8},{1,9},{2,10},{3,11},{4,12},{5,13},{6,14},{7,15},{8,16},{9,17... | collective-permute-start | bytes 1572872 | tf_op jit(solution)/shard_map/ppermute | solution.py:12
  512.5 32.0 %collective-permute-start.14 = (f32[4,256,128]{2,1,0:T(8,128)S(1)}, f32[4,256,128]{2,1,0:T(8,128)S(1)}, u32[]{:S(2)}, u32[]{:S(2)}) collective-permute-start(f32[4,256,128]{2,1,0:T(8,128)S(1)} %broadcast_select_fusion.11), channel_id=1, source_target_pairs={{0,16},{1,17},{2,18},{3,19},{4,20},{5,21},{6,22},{7,23},{8,24},{9,... | collective-permute-start | bytes 1572872 | tf_op jit(solution)/shard_map/ppermute | solution.py:12
  544.6 16.9 %collective-permute-start.15 = (f32[4,256,128]{2,1,0:T(8,128)S(1)}, f32[4,256,128]{2,1,0:T(8,128)S(1)}, u32[]{:S(2)}, u32[]{:S(2)}) collective-permute-start(f32[4,256,128]{2,1,0:T(8,128)S(1)} %broadcast_select_fusion.12), channel_id=1, source_target_pairs={{0,32},{1,33},{2,34},{3,35},{4,36},{5,37},{6,38},{7,39},{8,40},{9,... | collective-permute-start | bytes 1572872 | tf_op jit(solution)/shard_map/ppermute | solution.py:12
  561.6 1.0 copy-start.1
Sparse Core Ops, SparseCore 0:
  562.7 90.9 all-reduce.4
where the time goes:
time: 665 us; the launch traced here: 663 us
  waiting for transfers between devices  345 us (52%)
  other arithmetic  165 us (25%)
  starting transfers between devices  118 us (18%)
  local copies, waits for them, and re-layouts  19.8 us (3%)
  between operations  14.4 us (2%)
    ppermute x12, waiting for transfers between devices, from_behind(): return lax.ppermute(value, axis, pairs)  161 us
    unnamed x2, waiting for transfers between devices  90.5 us
    ppermute x8, waiting for transfers between devices, extended(): after = lax.ppermute(initial, axis, down)  84.6 us
    add x4, other arithmetic, adjoint(): return ((now, after, image + after * lap_fwd), None)  76.8 us
    ppermute x12, starting transfers between devices, from_behind(): return lax.ppermute(value, axis, pairs)  51.8 us
    ppermute x8, starting transfers between devices, extended(): before = lax.ppermute(last, axis, up)  39.4 us
    concatenate x8, other arithmetic, extended(): array = jnp.concatenate([before, array, after], axis=dim)  34.3 us
    dynamic_update_slice x4, other arithmetic, body(): _, laps = lax.scan(forward, (start, start), jnp.transpose(wavelet))  28.7 us
  transfers between devices with their start and end apart: 29, of which 29 were waited for; matrix products, arithmetic and copies ran while one was open for 0% of the time, Pallas kernels for 0%

commit v1 on v0

v1 whole, which is shorter than its diff:
```python
import functools

import jax
import jax.numpy as jnp
import numpy as np
from jax import lax
from jax.experimental import pallas as pl
from jax.experimental.pallas import tpu as pltpu
from jax.sharding import PartitionSpec as P

SCALE = 5040 / 128
COEFS = (None, 63.0, -7.875, 1.0, -0.0703125)
CENTER_Y, CENTER_Z = -336.0, -0.328125
CX, CY, CZ, STEPS = 4, 256, 128, 4
KINDS = 3 + STEPS
ROWS = KINDS * CX * (CY // 128)
WINDOW = 8
LAYERS = (WINDOW + 1) * CX


def band(size, center):
    apart = np.abs(np.arange(size)[:, None] - np.arange(size)[None, :])
    out = np.where(apart == 0, np.float32(center), np.float32(0))
    for k in range(1, 5):
        out[apart == k] = COEFS[k]
    return out.astype(jnp.bfloat16)


def ring(value, steps, axis="space"):
    count = lax.axis_size(axis)
    return lax.ppermute(value, axis, [(i, (i + steps) % count) for i in range(count)])


def either_way(value, steps):
    count = lax.axis_size("space")
    return lax.ppermute(
        value, "space", [(i, (i + (steps if i % 2 == 0 else -steps)) % count) for i in range(count)]
    )


def swap(value):
    count = lax.axis_size("space")
    return lax.ppermute(value, "space", [(i, i ^ 1) for i in range(count)])


def base_of(gap):
    return lambda w: CX * w + jnp.where(w >= gap, CX, 0)


def fetch(pairs, sems):
    copies = [pltpu.make_async_copy(src, dst, sems.at[i]) for i, (src, dst) in enumerate(pairs)]
    for copy in copies:
        copy.start()
    return copies


def fill_depths(depths):
    depths[...] = lax.broadcasted_iota(jnp.int32, (CZ, 128), 0).astype(jnp.float32)


def put(depths, term, z):
    return jnp.where(depths[pl.ds(z, 16), :] == term[1], term[0], 0.0)


def along(field, b, l, dy, dz, yz):
    f = field[b + l]
    high = f.astype(jnp.bfloat16)
    low = (f - high.astype(jnp.float32)).astype(jnp.bfloat16)
    r = jnp.dot(jnp.concatenate([high, low], 1), dy[...], preferred_element_type=jnp.float32)
    stack = jnp.concatenate([high, low], 0)
    yz[l] = r + jnp.dot(dz[...], stack, preferred_element_type=jnp.float32)


def across(field, b, n, yz, take):
    h, z = n // 8, 16 * (n % 8)
    at = (pl.ds(z, 16), pl.ds(128 * h, 128))
    x = [field[(b - 4 + i,) + at] for i in range(3 * CX)]
    for l in range(CX):
        lap = yz[(l,) + at]
        for k in range(1, 5):
            pair = x[4 + l + k] + x[4 + l - k]
            lap = lap + (pair if COEFS[k] == 1.0 else COEFS[k] * pair)
        take(l, h, z, at, x[4 + l], lap)


def sweep(u, w, low, high, place, dy, dz, yzu, yzw, take_u, take_w):
    def tile(t, _):
        b = place(t)
        for l in range(CX):
            along(u, b, l, dy, dz, yzu)
        take = take_u(t, b)
        for l in range(CX):
            along(w, b, l, dy, dz, yzw)
            for n in range(4 * l, 4 * l + 4):
                across(u, b, n, yzu, take)
        take = take_w(t, b)
        for n in range(16):
            across(w, b, n, yzw, take)
        return 0

    lax.fori_loop(low, high, tile, 0)


def first_kernel(
    numbers, amps, dy, dz, middle, a1, a2, a3, a4, others, lap_u, lap_w, comp,
    fu, fw, yzu, yzw, depths, sems,
):
    gap, start, core = numbers[0], numbers[1], numbers[2]
    base = base_of(gap)
    sign = 2 * core - 1
    pairs = [(middle.at[:, core], comp.at[pl.ds(8, 2)])]
    for i, ref in enumerate((a1, a2, a3, a4)):
        far = 2 * (i + 1) * sign
        pairs.append((ref.at[:, core], comp.at[pl.ds(8 + far, 2)]))
        pairs.append((others.at[i], comp.at[pl.ds(8 - far, 2)]))
    copies = fetch(pairs, sems)
    fill_depths(depths)
    for field in (fu, fw):
        field[pl.ds(CX * gap, CX)] = jnp.zeros((CX, CZ, CY), jnp.float32)
    for copy in copies:
        copy.wait()

    def row(w, kind, l, h):
        return comp[w + start, pl.ds((kind * CX + l) * 2 + h, 1), :]

    def fill(w, _):
        b = base(w)
        for l in range(CX):
            for h in range(2):
                u = (amps[0] * row(w, 0, l, h), row(w, 1, l, h))
                v = (row(w, 6, l, h), row(w, 2, l, h))
                for z in range(0, CZ, 16):
                    at = (b + l, pl.ds(z, 16), pl.ds(128 * h, 128))
                    fu[at] = put(depths, u, z)
                    fw[at] = put(depths, v, z)
        return 0

    lax.fori_loop(0, WINDOW, fill, 0)

    def keep(out):
        def at_tile(w, b):
            def take(l, h, z, at, now, lap):
                out[(w - 1, l) + at] = lap

            return take

        return at_tile

    sweep(fu, fw, 1, WINDOW - 1, base, dy, dz, yzu, yzw, keep(lap_u), keep(lap_w))


def second_kernel(
    numbers, amps, dy, dz, c0, c1, c2, c3, c4, c5, comp, lap_u, lap_w,
    out0, out1, coeff, u2, u3, w2, w3, lap2, lap3, yzu, yzw, image, depths, still, sems,
):
    gap, start, core = numbers[0], numbers[1], numbers[2]
    base = base_of(gap)
    tiles = (c0, c1, c2, c3, c4, c5)
    pairs = [(ref, coeff.at[jnp.bitwise_xor(i, core)]) for i, ref in enumerate(tiles)]
    copies = fetch(pairs, sems)
    fill_depths(depths)
    still[...] = jnp.zeros_like(still)
    for field in (u2, u3, w2, w3):
        field[pl.ds(CX * gap, CX)] = jnp.zeros((CX, CZ, CY), jnp.float32)
    for copy in copies:
        copy.wait()

    def row(w, kind, l, h):
        return comp[w + start, pl.ds((kind * CX + l) * 2 + h, 1), :]

    def source(w, amp):
        return {(l, h): (amp * row(w, 0, l, h), row(w, 1, l, h)) for l in range(CX) for h in range(2)}

    def trace(w, *scales):
        terms = {}
        for l in range(CX):
            for h in range(2):
                value = None
                for n, scale in scales:
                    r = row(w, 3 + n, l, h)
                    r = r if scale == 1 else scale * r
                    value = r if value is None else value + r
                terms[l, h] = (value, row(w, 2, l, h))
        return terms

    def second(w, _):
        b = base(w)
        su = source(w, 2.0 * amps[0] + amps[1])
        sw = trace(w, (3, 2.0), (2, 1))
        for l in range(CX):
            for h in range(2):
                for z in range(0, CZ, 16):
                    at = (pl.ds(z, 16), pl.ds(128 * h, 128))
                    c = coeff[(w - 1, l) + at]
                    u2[(b + l,) + at] = c * lap_u[(w - 1, l) + at] + put(depths, su[l, h], z)
                    w2[(b + l,) + at] = c * lap_w[(w - 1, l) + at] + put(depths, sw[l, h], z)
        return 0

    lax.fori_loop(1, WINDOW - 1, second, 0)

    def third_u(w, b):
        terms = source(w, amps[2] - amps[0])

        def take(l, h, z, at, now, lap):
            lap2[(w - 2, l) + at] = lap
            u3[(b + l,) + at] = 2.0 * now + coeff[(w - 1, l) + at] * lap + put(depths, terms[l, h], z)

        return take

    def third_w(w, b):
        terms = trace(w, (3, -1.0), (1, 1))

        def take(l, h, z, at, now, lap):
            w3[(b + l,) + at] = 2.0 * now + coeff[(w - 1, l) + at] * lap + put(depths, terms[l, h], z)

        return take

    sweep(u2, w2, 2, WINDOW - 2, base, dy, dz, yzu, yzw, third_u, third_w)

    def last_u(w, b):
        def take(l, h, z, at, now, lap):
            lap3[(w - 3, l) + at] = lap

        return take

    def last_w(w, b):
        ones, fours = trace(w, (3, 1)), trace(w, (0, 1))

        def take(l, h, z, at, now, lap):
            before = w2[(b + l,) + at]
            w4 = 2.0 * now - before + coeff[(w - 1, l) + at] * lap + put(depths, fours[l, h], z)
            total = put(depths, ones[l, h], z) * lap3[(w - 3, l) + at] + before * lap2[(w - 2, l) + at]
            image[(w - 3, l) + at] = total + now * lap_u[(w - 1, l) + at] + w4 * still[...]

        return take

    sweep(u3, w3, 3, WINDOW - 3, base, dy, dz, yzu, yzw, last_u, last_w)
    for l in range(CX):
        out0[l] = image[core, l].T
        out1[l] = image[1 - core, l].T


FIELD = (CZ, CY)
BLOCKS = 9


def matrices():
    dy, dz = band(CY, CENTER_Y), band(CZ, CENTER_Z)
    return jnp.asarray(np.concatenate([dy, dy], 0)), jnp.asarray(np.concatenate([dz, dz], 1))


def scratch(*lead):
    return pltpu.VMEM(lead + FIELD, jnp.float32)


def run_first(numbers, amps, surface):
    vmem = pl.BlockSpec(memory_space=pltpu.VMEM)
    smem = pl.BlockSpec(memory_space=pltpu.SMEM)
    anywhere = pl.BlockSpec(memory_space=pl.ANY)
    lap = jax.ShapeDtypeStruct((6, CX) + FIELD, jnp.float32)
    return pl.pallas_call(
        first_kernel,
        out_shape=(lap, lap, jax.ShapeDtypeStruct((2 * BLOCKS, ROWS, 128), jnp.float32)),
        in_specs=[smem, smem, vmem, vmem] + [anywhere] * 6,
        out_specs=(vmem, vmem, vmem),
        scratch_shapes=[
            scratch(LAYERS), scratch(LAYERS), scratch(CX), scratch(CX),
            pltpu.VMEM((CZ, 128), jnp.float32), pltpu.SemaphoreType.DMA((9,)),
        ],
        compiler_params=pltpu.CompilerParams(vmem_limit_bytes=28 * 2**20),
        cost_estimate=pl.CostEstimate(flops=10**6, bytes_accessed=2**20, transcendentals=0),
    )(numbers, amps, *matrices(), *surface)


def run_second(numbers, amps, coeffs, comp, lap_u, lap_w):
    vmem = pl.BlockSpec(memory_space=pltpu.VMEM)
    smem = pl.BlockSpec(memory_space=pltpu.SMEM)
    anywhere = pl.BlockSpec(memory_space=pl.ANY)
    out = jax.ShapeDtypeStruct((CX, CY, CZ), jnp.float32)
    return pl.pallas_call(
        second_kernel,
        out_shape=(out, out),
        in_specs=[smem, smem, vmem, vmem] + [anywhere] * 6 + [vmem] * 3,
        out_specs=(vmem, vmem),
        scratch_shapes=[
            scratch(6, CX),
            scratch(LAYERS), scratch(LAYERS), scratch(LAYERS), scratch(LAYERS),
            scratch(4, CX), scratch(2, CX), scratch(CX), scratch(CX), scratch(2, CX),
            pltpu.VMEM((CZ, 128), jnp.float32), pltpu.VMEM((16, 128), jnp.float32),
            pltpu.SemaphoreType.DMA((6,)),
        ],
        compiler_params=pltpu.CompilerParams(vmem_limit_bytes=40 * 2**20),
        cost_estimate=pl.CostEstimate(flops=9 * 10**9, bytes_accessed=12 * 2**20, transcendentals=0),
    )(numbers, amps, *matrices(), *coeffs, comp, lap_u, lap_w)


def body(model_velocity, first_tile, src_weight, src_depth, wavelet, rec_depth, residual):
    width = lax.axis_size("space")
    groups = lax.axis_size("shot")
    group = lax.axis_index("shot")
    place = lax.axis_index("space")
    core = place % 2
    anchor = first_tile[0]

    def slot_of(o):
        return jnp.where(place >= o % width, o // width, o // width + 1)

    slot = slot_of(anchor)

    velocity = lax.dynamic_index_in_dim(model_velocity, slot, 0, keepdims=False)[0]
    own = ((0.1 * velocity) ** 2 * (1.0 / SCALE)).transpose(0, 2, 1)

    kinds = [src_weight, src_depth.astype(jnp.float32), rec_depth.astype(jnp.float32)]
    kinds += [residual[:, n] for n in range(STEPS)]
    surface = jnp.stack(kinds, 1).reshape(2, ROWS, 128)
    first = core == 0

    def both(value):
        other = swap(value)
        return jnp.where(first, value, other), jnp.where(first, other, value)

    chips = (anchor // 2) % (width // 2)
    dy = chips % 4
    dz = chips // 4 + jnp.where(dy == 3, 1, 0)
    dy = jnp.where(dy == 3, -1, dy)
    dz = (dz + 3) % 8 - 3
    far = jnp.where(dz >= 2, 1, jnp.where(dz <= -2, -1, 0))
    near = dz - 3 * far

    def turn(value, digit, steps):
        up, down = both(either_way(value, steps))
        return jnp.where(digit == 1, up, jnp.where(digit == -1, down, value))

    block = jnp.stack(both(surface))
    block = turn(block, far, 24)
    block = turn(block, near, 8)

    ours = [either_way(block, 2 * q) for q in range(1, 5)]
    ours[3], own = lax.optimization_barrier((ours[3], own))
    left, right = ring(own, 2), ring(own, -2)
    others = jnp.stack([lax.dynamic_index_in_dim(value, 1 - core, 1, keepdims=False) for value in ours])
    blocks = [block] + ours + [swap(others)]
    cut = (anchor - (place - core - 3)) % width
    gap = jnp.where((cut >= 1) & (cut < WINDOW), cut, WINDOW)
    numbers = jnp.stack([gap, 5 - 2 * dy - anchor % 2, core]).astype(jnp.int32)
    amps = lax.dynamic_index_in_dim(wavelet, core, 0, keepdims=False)
    lap_u, lap_w, comp = run_first(numbers, amps, blocks)
    left, right, lap_u = lax.optimization_barrier((left, right, lap_u))

    coeffs = (left, swap(left), own, swap(own), right, swap(right))
    mine, theirs = run_second(numbers, amps, coeffs, comp, lap_u, lap_w)
    local = (0.02 / SCALE) * velocity * (mine + swap(theirs))

    flag = jnp.full((CX, 8, CZ), slot, jnp.int32).astype(jnp.float32)
    local = jnp.concatenate([local, flag], 1)
    total = None
    for d in range(groups):
        piece = lax.dynamic_index_in_dim(local, (group + d) % groups, 0, keepdims=False)
        if d:
            piece = ring(piece, d, "shot")
        at = piece[CY : CY + 1]
        both = jnp.stack([jnp.where(at == s, piece[:CY], 0.0) for s in range(2)])
        total = both if total is None else total + both
    return total[:, None, None]


def solution(mesh):
    placed = (
        P(None, "space", None, None, None),
        P("shot"),
        P("shot", "space", None),
        P("shot", "space", None),
        P("shot", None),
        P("shot", "space", None),
        P("shot", None, "space", None),
    )
    return jax.shard_map(
        body,
        mesh=mesh,
        in_specs=placed,
        out_specs=P(None, "space", "shot", None, None),
        check_vma=False,
    )
```

time: 665 us -> 81.4 us (0.12)
  waiting for transfers between devices: 345 us -> 26.8 us
  other arithmetic: 165 us -> 3.9 us
  starting transfers between devices: 118 us -> 31.9 us
  local copies, waits for them, and re-layouts: 19.8 us -> 1.59 us
  Pallas kernels: 0 us -> 16.1 us
  between operations: 14.4 us -> 1 us
    ppermute x28 -> x19, waiting for transfers between devices: 254 us -> 26.8 us  [the longest x5 13.5 us: ring(): lax.ppermute(value, axis, [(i, (i + steps) % count) for i in range(count)])]
    unnamed x2 -> x0, waiting for transfers between devices: 90.5 us -> none
    add x8 -> x1, other arithmetic: 89.3 us -> 0.07 us  [body(): total = both if total is None else total + both]
    ppermute x28 -> x19, starting transfers between devices: 118 us -> 31.9 us  [the longest x6 16.2 us: either_way(): lax.ppermute(value, 'space', [(i, (i + (steps if i % 2 == 0 else -steps))...]
    concatenate x8 -> x0, other arithmetic: 34.3 us -> none  [extended(): array = jnp.concatenate([before, array, after], axis=dim)]
    dynamic_update_slice x5 -> x0, other arithmetic: 28.8 us -> none  [the longest x4 28.7 us: body(): _, laps = lax.scan(forward, (start, start), jnp.transpose(wavelet))]
    pallas_call x0 -> x2, Pallas kernels: none -> 16.1 us  [the longest x1 9.42 us: run_second(): pl.pallas_call(second_kernel, out_shape=(out, out), in_specs=[smem, smem,...]
    while x8 -> x0, other arithmetic: 7.96 us -> none
  transfers between devices with their start and end apart: 29 -> 19, of which waited for: 29 -> 13; matrix products, arithmetic and copies ran while one was open for 0% -> 1% of each run, Pallas kernels for 0% -> 8%
where the time goes in v1:
time: 81.4 us; the launch traced here: 81.2 us
  starting transfers between devices  31.9 us (39%)
  waiting for transfers between devices  26.8 us (33%)
  Pallas kernels  16.1 us (20%)
  other arithmetic  3.9 us (5%)
  local copies, waits for them, and re-layouts  1.59 us (2%)
  between operations  1 us (1%)
    ppermute x6, starting transfers between devices, either_way(): lax.ppermute(value, 'space', [(i, (i + (steps if i % 2 == 0 else -steps))...  16.2 us
    ppermute x5, waiting for transfers between devices, ring(): lax.ppermute(value, axis, [(i, (i + steps) % count) for i in range(count)])  13.5 us
    pallas_call x1, Pallas kernels, run_second(): pl.pallas_call(second_kernel, out_shape=(out, out), in_specs=[smem, smem,...  9.42 us
    ppermute x5, starting transfers between devices, ring(): lax.ppermute(value, axis, [(i, (i + steps) % count) for i in range(count)])  8.49 us
    ppermute x8, starting transfers between devices, swap(): return lax.ppermute(value, 'space', [(i, i ^ 1) for i in range(count)])  7.19 us
    ppermute x8, waiting for transfers between devices, swap(): return lax.ppermute(value, 'space', [(i, i ^ 1) for i in range(count)])  6.95 us
    pallas_call x1, Pallas kernels, run_first(): pl.pallas_call(first_kernel, out_shape=(lap, lap, jax.ShapeDtypeStruct((2...  6.65 us
    ppermute x6, waiting for transfers between devices, either_way(): lax.ppermute(value, 'space', [(i, (i + (steps if i % 2 == 0 else -steps))...  6.34 us
  transfers between devices with their start and end apart: 19, of which 13 were waited for; matrix products, arithmetic and copies ran while one was open for 1% of the time, Pallas kernels for 8%

profile of v1, /device:TPU:1, one launch (start us, length us, event | category | flops | bytes accessed | tf_op | source)
XLA Modules:
  0.0 81.2 jit_solution(8832063912234026702)
XLA Ops:
  0.0 0.0 copy-start
  0.0 0.0 copy-start.4
  0.0 0.8 %convert_bitcast_fusion = (f32[2,1,4,256]{3,2,1,0:T(4,128)S(1)}, f32[2,1,4,256]{3,2,1,0:T(4,128)S(1)}) fusion(s32[2,4,256]{2,1,0:T(4,128)} %param.16, s32[2,4,256]{2,1,0:T(4,128)} %param.14), kind=kLoop, calls=%fused_computation.40 | loop fusion | flops 4096 | bytes 32768 | tf_op jit(solution)/shard_map/stack | solution.py:315
  0.9 0.8 pad_maximum_fusion.2
  1.7 3.3 %collective-permute-start = (f32[2,56,128]{2,1,0:T(8,128)S(1)}, f32[2,56,128]{2,1,0:T(8,128)S(1)}, u32[]{:S(2)}, u32[]{:S(2)}) collective-permute-start(f32[2,56,128]{2,1,0:T(8,128)S(1)} %reshape.166), channel_id=1, source_target_pairs={{0,1},{1,0},{2,3},{3,2},{4,5},{5,4},{6,7},{7,6},{8,9},{9,8},{10,11... | collective-permute-start | bytes 172040 | tf_op jit(solution)/shard_map/ppermute | solution.py:43
  5.0 0.9 %collective-permute-done = f32[2,56,128]{2,1,0:T(8,128)S(1)} collective-permute-done((f32[2,56,128]{2,1,0:T(8,128)S(1)}, f32[2,56,128]{2,1,0:T(8,128)S(1)}, u32[]{:S(2)}, u32[]{:S(2)}) %collective-permute-start) | collective-permute-done | bytes 57376 | tf_op jit(solution)/shard_map/ppermute | solution.py:43
  5.9 4.8 %collective-permute-start.1 = (f32[2,2,56,128]{3,2,1,0:T(8,128)S(1)}, f32[2,2,56,128]{3,2,1,0:T(8,128)S(1)}, u32[]{:S(2)}, u32[]{:S(2)}) collective-permute-start(f32[2,2,56,128]{3,2,1,0:T(8,128)S(1)} %pad_maximum_fusion.1), channel_id=1, source_target_pairs={{0,24},{1,41},{2,26},{3,43},{4,28},{5,45},{6,30},{7,47},{8,32},{9,... | collective-permute-start | bytes 344072 | tf_op jit(solution)/shard_map/ppermute | solution.py:36
  10.7 4.2 %collective-permute-done.1 = f32[2,2,56,128]{3,2,1,0:T(8,128)S(1)} collective-permute-done((f32[2,2,56,128]{3,2,1,0:T(8,128)S(1)}, f32[2,2,56,128]{3,2,1,0:T(8,128)S(1)}, u32[]{:S(2)}, u32[]{:S(2)}) %collective-permute-start.1) | collective-permute-done | bytes 114720 | tf_op jit(solution)/shard_map/ppermute | solution.py:36
  14.9 0.0 collective-permute-start.2
  15.7 0.6 collective-permute-done.2
  16.3 1.8 %collective-permute-start.3 = (f32[2,2,56,128]{3,2,1,0:T(8,128)S(1)}, f32[2,2,56,128]{3,2,1,0:T(8,128)S(1)}, u32[]{:S(2)}, u32[]{:S(2)}) collective-permute-start(f32[2,2,56,128]{3,2,1,0:T(8,128)S(1)} %select_select_fusion.1), channel_id=1, source_target_pairs={{0,8},{1,57},{2,10},{3,59},{4,12},{5,61},{6,14},{7,63},{8,16},{9,1... | collective-permute-start | bytes 344072 | tf_op jit(solution)/shard_map/ppermute | solution.py:36
  18.1 1.9 %collective-permute-done.3 = f32[2,2,56,128]{3,2,1,0:T(8,128)S(1)} collective-permute-done((f32[2,2,56,128]{3,2,1,0:T(8,128)S(1)}, f32[2,2,56,128]{3,2,1,0:T(8,128)S(1)}, u32[]{:S(2)}, u32[]{:S(2)}) %collective-permute-start.3) | collective-permute-done | bytes 114720 | tf_op jit(solution)/shard_map/ppermute | solution.py:36
  20.0 2.5 %collective-permute-start.4 = (f32[2,2,56,128]{3,2,1,0:T(8,128)S(1)}, f32[2,2,56,128]{3,2,1,0:T(8,128)S(1)}, u32[]{:S(2)}, u32[]{:S(2)}) collective-permute-start(f32[2,2,56,128]{3,2,1,0:T(8,128)S(1)} %collective-permute-done.3), channel_id=1, source_target_pairs={{0,1},{1,0},{2,3},{3,2},{4,5},{5,4},{6,7},{7,6},{8,9},{9,8},{10,11... | collective-permute-start | bytes 344072 | tf_op jit(solution)/shard_map/ppermute | solution.py:43
  22.5 0.0 copy-done
  22.5 0.2 copy.20
  22.7 0.0 copy-start.3
  22.8 0.7 collective-permute-done.4
  23.5 3.2 %collective-permute-start.5 = (f32[2,2,56,128]{3,2,1,0:T(8,128)S(1)}, f32[2,2,56,128]{3,2,1,0:T(8,128)S(1)}, u32[]{:S(2)}, u32[]{:S(2)}) collective-permute-start(f32[2,2,56,128]{3,2,1,0:T(8,128)S(1)} %select_select_fusion.middle), channel_id=1, source_target_pairs={{0,8},{1,57},{2,10},{3,59},{4,12},{5,61},{6,14},{7,63},{8,16},{9,1... | collective-permute-start | bytes 344072 | tf_op jit(solution)/shard_map/ppermute | solution.py:36
  26.7 2.8 %collective-permute-start.10 = (f32[2,2,56,128]{3,2,1,0:T(8,128)S(1)}, f32[2,2,56,128]{3,2,1,0:T(8,128)S(1)}, u32[]{:S(2)}, u32[]{:S(2)}) collective-permute-start(f32[2,2,56,128]{3,2,1,0:T(8,128)S(1)} %select_select_fusion.middle), channel_id=1, source_target_pairs={{0,6},{1,59},{2,8},{3,61},{4,10},{5,63},{6,12},{7,1},{8,14},{9,3},... | collective-permute-start | bytes 344072 | tf_op jit(solution)/shard_map/ppermute | solution.py:36
  29.5 0.1 multiply_bitcast_fusion.c2
  29.6 2.5 %collective-permute-start.9 = (f32[2,2,56,128]{3,2,1,0:T(8,128)S(1)}, f32[2,2,56,128]{3,2,1,0:T(8,128)S(1)}, u32[]{:S(2)}, u32[]{:S(2)}) collective-permute-start(f32[2,2,56,128]{3,2,1,0:T(8,128)S(1)} %select_select_fusion.middle), channel_id=1, source_target_pairs={{0,4},{1,61},{2,6},{3,63},{4,8},{5,1},{6,10},{7,3},{8,12},{9,5},{1... | collective-permute-start | bytes 344072 | tf_op jit(solution)/shard_map/ppermute | solution.py:36
  32.1 1.1 %collective-permute-start.8 = (f32[2,2,56,128]{3,2,1,0:T(8,128)S(1)}, f32[2,2,56,128]{3,2,1,0:T(8,128)S(1)}, u32[]{:S(2)}, u32[]{:S(2)}) collective-permute-start(f32[2,2,56,128]{3,2,1,0:T(8,128)S(1)} %select_select_fusion.middle), channel_id=1, source_target_pairs={{0,2},{1,63},{2,4},{3,1},{4,6},{5,3},{6,8},{7,5},{8,10},{9,7},{10,... | collective-permute-start | bytes 344072 | tf_op jit(solution)/shard_map/ppermute | solution.py:36
  33.1 0.0 copy-done.3
  33.1 0.0 collective-permute-done.5.a4
  33.1 0.4 collective-permute-start.6
  33.5 4.4 %collective-permute-start.7 = (f32[4,128,256]{2,1,0:T(8,128)S(1)}, f32[4,128,256]{2,1,0:T(8,128)}, u32[]{:S(2)}, u32[]{:S(2)}) collective-permute-start(f32[4,128,256]{2,1,0:T(8,128)S(1)} %multiply_bitcast_fusion.c2), channel_id=1, source_target_pairs={{0,62},{1,63},{2,0},{3,1},{4,2},{5,3},{6,4},{7,5},{8,6},{9,7},{10,... | collective-permute-start | bytes 1572872 | tf_op jit(solution)/shard_map/ppermute | solution.py:31
  37.9 0.0 collective-permute-done.10.a3
  37.9 0.3 collective-permute-done.9.a2
  38.2 0.0 collective-permute-done.8.a1
  38.3 0.2 collective-permute-start.11
  38.4 0.0 copy-done.4
  38.5 0.1 pad_add_fusion.numbers
  38.5 0.4 collective-permute-start.13
  39.0 0.9 %collective-permute-done.11.others = f32[4,2,56,128]{3,2,1,0:T(8,128)S(1)} collective-permute-done((f32[4,2,56,128]{3,2,1,0:T(8,128)S(1)}, f32[4,2,56,128]{3,2,1,0:T(8,128)S(1)}, u32[]{:S(2)}, u32[]{:S(2)}) %collective-permute-start.11) | collective-permute-done | bytes 229408 | tf_op jit(solution)/shard_map/ppermute | solution.py:43
  39.9 6.7 %shard_map.109 = (f32[6,4,128,256]{3,2,1,0:T(8,128)S(1)}, f32[6,4,128,256]{3,2,1,0:T(8,128)S(1)}, f32[18,56,128]{2,1,0:T(8,128)S(1)}) custom-call(s32[3]{0:T(128)S(1)} %pad_add_fusion.numbers, f32[4]{0:T(128)S(1)} %fusion.5.amps, bf16[512,256]{1,0:T(8,128)(2,1)S(1)} %copy-done.1, bf16[128,256]{1,0:T(8,128)(2,1)S(1)} %copy-done.2, ...), custom_call_target="tpu_custom_call" | custom-call | flops 1000000 | bytes 1048576 | tf_op jit(solution)/shard_map/pallas_call | solution.py:261
  46.5 2.5 %collective-permute-done.6.c0 = f32[4,128,256]{2,1,0:T(8,128)S(1)} collective-permute-done((f32[4,128,256]{2,1,0:T(8,128)S(1)}, f32[4,128,256]{2,1,0:T(8,128)S(1)}, u32[]{:S(2)}, u32[]{:S(2)}) %collective-permute-start.6) | collective-permute-done | bytes 524320 | tf_op jit(solution)/shard_map/ppermute | solution.py:31
  49.1 0.0 collective-permute-done.7.c4
  49.1 0.0 collective-permute-start.12
  49.1 0.5 collective-permute-start.14
  49.6 0.0 collective-permute-done.13.c3
  49.6 2.1 %collective-permute-done.12.c1 = f32[4,128,256]{2,1,0:T(8,128)S(1)} collective-permute-done((f32[4,128,256]{2,1,0:T(8,128)S(1)}, f32[4,128,256]{2,1,0:T(8,128)S(1)}, u32[]{:S(2)}, u32[]{:S(2)}) %collective-permute-start.12) | collective-permute-done | bytes 524320 | tf_op jit(solution)/shard_map/ppermute | solution.py:43
  51.7 0.3 collective-permute-done.14.c5
  51.9 9.4 %shard_map.110 = (f32[4,256,128]{2,1,0:T(8,128)S(1)}, f32[4,256,128]{2,1,0:T(8,128)S(1)}) custom-call(s32[3]{0:T(128)S(1)} %pad_add_fusion.numbers, f32[4]{0:T(128)S(1)} %fusion.5.amps, bf16[512,256]{1,0:T(8,128)(2,1)S(1)} %copy-done.1, bf16[128,256]{1,0:T(8,128)(2,1)S(1)} %copy-done.2, f32[4,128,256]{2,1,0:T(8,128)S(1)} %collective-permute-done.6.c0, ...), custom_call_target="tpu_custom_call" | custom-call | flops 8999999488 | bytes 12582912 | tf_op jit(solution)/shard_map/pallas_call | solution.py:280
  61.4 0.2 copy.17
  61.6 0.2 collective-permute-start.15
  61.8 0.2 copy.18
  62.0 1.6 %collective-permute-done.15 = f32[4,256,128]{1,2,0:T(8,128)S(1)} collective-permute-done((f32[4,256,128]{1,2,0:T(8,128)S(1)}, f32[4,256,128]{1,2,0:T(8,128)S(1)}, u32[]{:S(2)}, u32[]{:S(2)}) %collective-permute-start.15) | collective-permute-done | bytes 524320 | tf_op jit(solution)/shard_map/ppermute | solution.py:43
  63.6 1.1 %bitcast_multiply_fusion = f32[4,256,128]{1,2,0:T(8,128)S(1)} fusion(f32[4,256,128]{1,2,0:T(8,128)S(1)} %copy.18, f32[4,256,128]{1,2,0:T(8,128)S(1)} %collective-permute-done.15, f32[1,1,4,256,128]{3,4,2,1,0:T(8,128)} %copy-done.3), kind=kLoop, calls=%fused_computation.5 | loop fusion | flops 393216 | bytes 2097152 | tf_op jit(solution)/shard_map/mul | solution.py:352
  64.8 2.5 %collective-permute-start.18 = (f32[264,128]{0,1:T(8,128)S(1)}, f32[264,128]{0,1:T(8,128)S(1)}, u32[]{:S(2)}, u32[]{:S(2)}) collective-permute-start(f32[264,128]{0,1:T(8,128)S(1)} %get-tuple-element.33), channel_id=1, source_target_pairs={{0,192},{64,0},{128,64},{192,128},{1,193},{65,1},{129,65},{193,129... | collective-permute-start | bytes 405512 | tf_op jit(solution)/shard_map/ppermute | solution.py:31
  67.3 0.5 collective-permute-start.17
  67.8 0.6 collective-permute-start.16
  68.5 0.1 compare_reduce_fusion.7
  68.6 0.1 select_bitcast_fusion.7
  68.7 6.8 %collective-permute-done.18 = f32[264,128]{0,1:T(8,128)S(1)} collective-permute-done((f32[264,128]{0,1:T(8,128)S(1)}, f32[264,128]{0,1:T(8,128)S(1)}, u32[]{:S(2)}, u32[]{:S(2)}) %collective-permute-start.18) | collective-permute-done | bytes 135200 | tf_op jit(solution)/shard_map/ppermute | solution.py:31
  75.5 0.1 compare_reduce_fusion.1
  75.7 0.0 collective-permute-done.17
  75.7 0.1 compare_reduce_fusion.3
  75.8 4.1 %collective-permute-done.16 = f32[264,128]{0,1:T(8,128)S(1)} collective-permute-done((f32[264,128]{0,1:T(8,128)S(1)}, f32[264,128]{0,1:T(8,128)S(1)}, u32[]{:S(2)}, u32[]{:S(2)}) %collective-permute-start.16) | collective-permute-done | bytes 135200 | tf_op jit(solution)/shard_map/ppermute | solution.py:31
  79.9 0.1 compare_reduce_fusion.5
  80.0 0.1 select_bitcast_fusion.1
  80.1 0.1 select_bitcast_fusion.3
  80.2 0.1 select_bitcast_fusion.5
  80.3 0.1 fusion.1
  80.4 0.8 %copy.19 = f32[2,1,1,256,128]{4,3,2,1,0:T(8,128)} copy(f32[2,1,1,256,128]{3,4,2,1,0:T(8,128)S(1)} %fusion.1) | data formatting | bytes 524288 | tf_op jit(solution)/shard_map/add | solution.py:363
  (17 shorter events, 0.2 us)
Async XLA Ops:
  0.0 22.5 %copy-start = (f32[2,1,4,256,128]{4,3,2,1,0:T(8,128)S(1)}, f32[2,1,4,256,128]{4,3,2,1,0:T(8,128)}, u32[]{:S(2)}) copy-start(f32[2,1,4,256,128]{4,3,2,1,0:T(8,128)} %param.11) | copy-start | bytes 3145732
  0.0 39.8 %copy-start.1 = (bf16[512,256]{1,0:T(8,128)(2,1)S(1)}, bf16[512,256]{1,0:T(8,128)(2,1)}, u32[]{:S(2)}) copy-start(bf16[512,256]{1,0:T(8,128)(2,1)} %constant.171.clone.dy) | copy-start | bytes 786436
  0.0 39.8 %copy-start.2 = (bf16[128,256]{1,0:T(8,128)(2,1)S(1)}, bf16[128,256]{1,0:T(8,128)(2,1)}, u32[]{:S(2)}) copy-start(bf16[128,256]{1,0:T(8,128)(2,1)} %constant.172.clone.dz) | copy-start | bytes 196612
  0.0 38.4 %copy-start.4 = (f32[2,4]{1,0:T(2,128)S(1)}, f32[2,4]{1,0:T(2,128)}, u32[]{:S(2)}) copy-start(f32[2,4]{1,0:T(2,128)} %param.15) | copy-start | bytes 100
  1.7 4.2 %collective-permute-start = (f32[2,56,128]{2,1,0:T(8,128)S(1)}, f32[2,56,128]{2,1,0:T(8,128)S(1)}, u32[]{:S(2)}, u32[]{:S(2)}) collective-permute-start(f32[2,56,128]{2,1,0:T(8,128)S(1)} %reshape.166), channel_id=1, source_target_pairs={{0,1},{1,0},{2,3},{3,2},{4,5},{5,4},{6,7},{7,6},{8,9},{9,8},{10,11... | collective-permute-start | bytes 172040 | tf_op jit(solution)/shard_map/ppermute | solution.py:43
  5.9 9.0 %collective-permute-start.1 = (f32[2,2,56,128]{3,2,1,0:T(8,128)S(1)}, f32[2,2,56,128]{3,2,1,0:T(8,128)S(1)}, u32[]{:S(2)}, u32[]{:S(2)}) collective-permute-start(f32[2,2,56,128]{3,2,1,0:T(8,128)S(1)} %pad_maximum_fusion.1), channel_id=1, source_target_pairs={{0,24},{1,41},{2,26},{3,43},{4,28},{5,45},{6,30},{7,47},{8,32},{9,... | collective-permute-start | bytes 344072 | tf_op jit(solution)/shard_map/ppermute | solution.py:36
  14.9 1.3 %collective-permute-start.2 = (f32[2,2,56,128]{3,2,1,0:T(8,128)S(1)}, f32[2,2,56,128]{3,2,1,0:T(8,128)S(1)}, u32[]{:S(2)}, u32[]{:S(2)}) collective-permute-start(f32[2,2,56,128]{3,2,1,0:T(8,128)S(1)} %collective-permute-done.1), channel_id=1, source_target_pairs={{0,1},{1,0},{2,3},{3,2},{4,5},{5,4},{6,7},{7,6},{8,9},{9,8},{10,11... | collective-permute-start | bytes 344072 | tf_op jit(solution)/shard_map/ppermute | solution.py:43
  16.3 3.7 %collective-permute-start.3 = (f32[2,2,56,128]{3,2,1,0:T(8,128)S(1)}, f32[2,2,56,128]{3,2,1,0:T(8,128)S(1)}, u32[]{:S(2)}, u32[]{:S(2)}) collective-permute-start(f32[2,2,56,128]{3,2,1,0:T(8,128)S(1)} %select_select_fusion.1), channel_id=1, source_target_pairs={{0,8},{1,57},{2,10},{3,59},{4,12},{5,61},{6,14},{7,63},{8,16},{9,1... | collective-permute-start | bytes 344072 | tf_op jit(solution)/shard_map/ppermute | solution.py:36
  20.0 3.5 %collective-permute-start.4 = (f32[2,2,56,128]{3,2,1,0:T(8,128)S(1)}, f32[2,2,56,128]{3,2,1,0:T(8,128)S(1)}, u32[]{:S(2)}, u32[]{:S(2)}) collective-permute-start(f32[2,2,56,128]{3,2,1,0:T(8,128)S(1)} %collective-permute-done.3), channel_id=1, source_target_pairs={{0,1},{1,0},{2,3},{3,2},{4,5},{5,4},{6,7},{7,6},{8,9},{9,8},{10,11... | collective-permute-start | bytes 344072 | tf_op jit(solution)/shard_map/ppermute | solution.py:43
  22.7 10.4 %copy-start.3 = (f32[1,1,4,256,128]{3,4,2,1,0:T(8,128)}, f32[1,1,4,256,128]{3,4,2,1,0:T(8,128)S(1)}, u32[]{:S(2)}) copy-start(f32[1,1,4,256,128]{3,4,2,1,0:T(8,128)S(1)} %copy.20) | copy-start | bytes 1572868
  23.5 9.6 %collective-permute-start.5 = (f32[2,2,56,128]{3,2,1,0:T(8,128)S(1)}, f32[2,2,56,128]{3,2,1,0:T(8,128)S(1)}, u32[]{:S(2)}, u32[]{:S(2)}) collective-permute-start(f32[2,2,56,128]{3,2,1,0:T(8,128)S(1)} %select_select_fusion.middle), channel_id=1, source_target_pairs={{0,8},{1,57},{2,10},{3,59},{4,12},{5,61},{6,14},{7,63},{8,16},{9,1... | collective-permute-start | bytes 344072 | tf_op jit(solution)/shard_map/ppermute | solution.py:36
  26.7 11.2 %collective-permute-start.10 = (f32[2,2,56,128]{3,2,1,0:T(8,128)S(1)}, f32[2,2,56,128]{3,2,1,0:T(8,128)S(1)}, u32[]{:S(2)}, u32[]{:S(2)}) collective-permute-start(f32[2,2,56,128]{3,2,1,0:T(8,128)S(1)} %select_select_fusion.middle), channel_id=1, source_target_pairs={{0,6},{1,59},{2,8},{3,61},{4,10},{5,63},{6,12},{7,1},{8,14},{9,3},... | collective-permute-start | bytes 344072 | tf_op jit(solution)/shard_map/ppermute | solution.py:36
  29.6 8.7 %collective-permute-start.9 = (f32[2,2,56,128]{3,2,1,0:T(8,128)S(1)}, f32[2,2,56,128]{3,2,1,0:T(8,128)S(1)}, u32[]{:S(2)}, u32[]{:S(2)}) collective-permute-start(f32[2,2,56,128]{3,2,1,0:T(8,128)S(1)} %select_select_fusion.middle), channel_id=1, source_target_pairs={{0,4},{1,61},{2,6},{3,63},{4,8},{5,1},{6,10},{7,3},{8,12},{9,5},{1... | collective-permute-start | bytes 344072 | tf_op jit(solution)/shard_map/ppermute | solution.py:36
  32.1 6.2 %collective-permute-start.8 = (f32[2,2,56,128]{3,2,1,0:T(8,128)S(1)}, f32[2,2,56,128]{3,2,1,0:T(8,128)S(1)}, u32[]{:S(2)}, u32[]{:S(2)}) collective-permute-start(f32[2,2,56,128]{3,2,1,0:T(8,128)S(1)} %select_select_fusion.middle), channel_id=1, source_target_pairs={{0,2},{1,63},{2,4},{3,1},{4,6},{5,3},{6,8},{7,5},{8,10},{9,7},{10,... | collective-permute-start | bytes 344072 | tf_op jit(solution)/shard_map/ppermute | solution.py:36
  33.1 15.9 %collective-permute-start.6 = (f32[4,128,256]{2,1,0:T(8,128)S(1)}, f32[4,128,256]{2,1,0:T(8,128)S(1)}, u32[]{:S(2)}, u32[]{:S(2)}) collective-permute-start(f32[4,128,256]{2,1,0:T(8,128)S(1)} %multiply_bitcast_fusion.c2), channel_id=1, source_target_pairs={{0,2},{1,3},{2,4},{3,5},{4,6},{5,7},{6,8},{7,9},{8,10},{9,11},{10,... | collective-permute-start | bytes 1572872 | tf_op jit(solution)/shard_map/ppermute | solution.py:31
  33.5 15.5 %collective-permute-start.7 = (f32[4,128,256]{2,1,0:T(8,128)S(1)}, f32[4,128,256]{2,1,0:T(8,128)}, u32[]{:S(2)}, u32[]{:S(2)}) collective-permute-start(f32[4,128,256]{2,1,0:T(8,128)S(1)} %multiply_bitcast_fusion.c2), channel_id=1, source_target_pairs={{0,62},{1,63},{2,0},{3,1},{4,2},{5,3},{6,4},{7,5},{8,6},{9,7},{10,... | collective-permute-start | bytes 1572872 | tf_op jit(solution)/shard_map/ppermute | solution.py:31
  38.3 1.6 %collective-permute-start.11 = (f32[4,2,56,128]{3,2,1,0:T(8,128)S(1)}, f32[4,2,56,128]{3,2,1,0:T(8,128)S(1)}, u32[]{:S(2)}, u32[]{:S(2)}) collective-permute-start(f32[4,2,56,128]{3,2,1,0:T(8,128)S(1)} %pad_maximum_fusion), channel_id=1, source_target_pairs={{0,1},{1,0},{2,3},{3,2},{4,5},{5,4},{6,7},{7,6},{8,9},{9,8},{10,11... | collective-permute-start | bytes 688136 | tf_op jit(solution)/shard_map/ppermute | solution.py:43
  38.5 11.0 %collective-permute-start.13 = (f32[4,128,256]{2,1,0:T(8,128)S(1)}, f32[4,128,256]{2,1,0:T(8,128)S(1)}, u32[]{:S(2)}, u32[]{:S(2)}) collective-permute-start(f32[4,128,256]{2,1,0:T(8,128)S(1)} %multiply_bitcast_fusion.c2), channel_id=1, source_target_pairs={{0,1},{1,0},{2,3},{3,2},{4,5},{5,4},{6,7},{7,6},{8,9},{9,8},{10,11... | collective-permute-start | bytes 1572872 | tf_op jit(solution)/shard_map/ppermute | solution.py:43
  49.1 2.6 %collective-permute-start.12 = (f32[4,128,256]{2,1,0:T(8,128)S(1)}, f32[4,128,256]{2,1,0:T(8,128)S(1)}, u32[]{:S(2)}, u32[]{:S(2)}) collective-permute-start(f32[4,128,256]{2,1,0:T(8,128)S(1)} %collective-permute-done.6.c0), channel_id=1, source_target_pairs={{0,1},{1,0},{2,3},{3,2},{4,5},{5,4},{6,7},{7,6},{8,9},{9,8},{10,11... | collective-permute-start | bytes 1572872 | tf_op jit(solution)/shard_map/ppermute | solution.py:43
  49.1 2.9 %collective-permute-start.14 = (f32[4,128,256]{2,1,0:T(8,128)}, f32[4,128,256]{2,1,0:T(8,128)S(1)}, u32[]{:S(2)}, u32[]{:S(2)}) collective-permute-start(f32[4,128,256]{2,1,0:T(8,128)} %collective-permute-done.7.c4), channel_id=1, source_target_pairs={{0,1},{1,0},{2,3},{3,2},{4,5},{5,4},{6,7},{7,6},{8,9},{9,8},{10,11... | collective-permute-start | bytes 1572872 | tf_op jit(solution)/shard_map/ppermute | solution.py:43
  61.6 2.0 %collective-permute-start.15 = (f32[4,256,128]{1,2,0:T(8,128)S(1)}, f32[4,256,128]{1,2,0:T(8,128)S(1)}, u32[]{:S(2)}, u32[]{:S(2)}) collective-permute-start(f32[4,256,128]{1,2,0:T(8,128)S(1)} %copy.17), channel_id=1, source_target_pairs={{0,1},{1,0},{2,3},{3,2},{4,5},{5,4},{6,7},{7,6},{8,9},{9,8},{10,11... | collective-permute-start | bytes 1572872 | tf_op jit(solution)/shard_map/ppermute | solution.py:43
  64.8 10.8 %collective-permute-start.18 = (f32[264,128]{0,1:T(8,128)S(1)}, f32[264,128]{0,1:T(8,128)S(1)}, u32[]{:S(2)}, u32[]{:S(2)}) collective-permute-start(f32[264,128]{0,1:T(8,128)S(1)} %get-tuple-element.33), channel_id=1, source_target_pairs={{0,192},{64,0},{128,64},{192,128},{1,193},{65,1},{129,65},{193,129... | collective-permute-start | bytes 405512 | tf_op jit(solution)/shard_map/ppermute | solution.py:31
  67.3 8.3 %collective-permute-start.17 = (f32[264,128]{0,1:T(8,128)S(1)}, f32[264,128]{0,1:T(8,128)S(1)}, u32[]{:S(2)}, u32[]{:S(2)}) collective-permute-start(f32[264,128]{0,1:T(8,128)S(1)} %get-tuple-element.35), channel_id=1, source_target_pairs={{0,128},{64,192},{128,0},{192,64},{1,129},{65,193},{129,1},{193,65... | collective-permute-start | bytes 405512 | tf_op jit(solution)/shard_map/ppermute | solution.py:31
  67.8 12.0 %collective-permute-start.16 = (f32[264,128]{0,1:T(8,128)S(1)}, f32[264,128]{0,1:T(8,128)S(1)}, u32[]{:S(2)}, u32[]{:S(2)}) collective-permute-start(f32[264,128]{0,1:T(8,128)S(1)} %get-tuple-element.34), channel_id=1, source_target_pairs={{0,64},{64,128},{128,192},{192,0},{1,65},{65,129},{129,193},{193,1... | collective-permute-start | bytes 405512 | tf_op jit(solution)/shard_map/ppermute | solution.py:31
